TPU v7x, 32 devices: a whole 2x2x4 slice. The times are simulated.
32 devices in a mesh: pipe: 4 (over y, x), seq: 8 (over z, core).
Axes of the slice: x: 2, y: 2, z: 4, core: 2. Of those that a mesh axis runs over, the one named last changes fastest.
Arguments:
- inputs: bfloat16 [4, 2, 1024, 1024], P('pipe', None, 'seq'), may hold values from -6 to 6
- incoming: bfloat16 [4, 2, 1024, 1024], P('pipe', None, 'seq'), may hold values from -6 to 6
- angles: float32 [4, 2, 1024], P('pipe'), may hold values from -3.140625 to 3.140625
- level_weights: float32 [4, 11, 1024], P('pipe'), may hold values from -1.75 to 1.75
- mix_weight: bfloat16 [4, 1024, 2048], P('pipe'), may hold values from -0.1875 to 0.1875
Outputs:
- grad_input: bfloat16 [4, 2, 1024, 1024], P('pipe', None, 'seq')
- grad_angles: float32 [4, 2, 1024], P('pipe')
- grad_levels: float32 [4, 11, 1024], P('pipe')
- grad_mix: float32 [4, 1024, 2048], P('pipe', 'seq')
All inputs are finite; a program needn't handle non-finite values.
Results may differ from a plain program's by a relative error of at most 0.015.
Values may be sent and summed in bfloat16 or wider, within the bound.
A program may use at most 128 MiB of HBM per device.

v0:
```python
import jax
import jax.numpy as jnp
from jax import lax
from jax.sharding import PartitionSpec as P


def shifted_2(block, axis, distance):
    devices = range(lax.axis_size(axis))
    route = [(i - distance, i) for i in devices if i - distance in devices]
    return lax.ppermute(block, axis, route)


def shifted_3(value, axis, steps):
    count = lax.axis_size(axis)
    pairs = [(source, (source + steps) % count) for source in range(count)]
    return lax.ppermute(value, axis, pairs)


def rounded(values):
    return lax.optimization_barrier(values.astype(jnp.bfloat16))


def near_behind(state_now, spacing, positions):
    rim_rows = shifted_2(state_now[:, positions - spacing :, :], "seq", 1)
    return jnp.concatenate([rim_rows, state_now[:, : positions - spacing, :]], axis=1)


def tap_terms(totals, adjoint, weighted, current, previous):
    return (
        totals[0] + jnp.sum(adjoint * current, axis=(0, 1)),
        totals[1] + jnp.sum(adjoint * previous, axis=(0, 1)),
        totals[2] + jnp.sum(weighted * current, axis=(0, 1)),
        totals[3] + jnp.sum(weighted * previous, axis=(0, 1)),
    )


def shards(inputs, incoming, angles, level_weights, mix_weight):
    activations = inputs[0]
    sequences, positions, channels = activations.shape
    seq_devices = lax.axis_size("seq")
    levels = level_weights.shape[1] - 1
    near_count = positions.bit_length() - 1
    grad_scale = float(sequences * positions * seq_devices) ** (-0.5)
    weights = level_weights[0]
    w_mix = mix_weight[0]
    c_low = jnp.cos(angles[0, 0])
    s_low = jnp.sin(angles[0, 0])
    c_high = jnp.cos(angles[0, 1])
    s_high = jnp.sin(angles[0, 1])
    received = shifted_3(incoming, "pipe", -1)[0]
    states = []
    shifted_states = []
    mixed = jnp.zeros(activations.shape, jnp.float32)
    state_now = activations
    for level_idx in range(near_count):
        spacing = 2**level_idx
        shifted = near_behind(state_now, spacing, positions)
        current = state_now.astype(jnp.float32)
        previous = shifted.astype(jnp.float32)
        mixed = mixed + weights[level_idx] * (c_high * current + s_high * previous)
        states.append(state_now)
        shifted_states.append(shifted)
        state_now = rounded(c_low * current + s_low * previous)
    for level_idx in range(near_count, levels):
        spacing = 2**level_idx
        shifted = shifted_2(state_now, "seq", spacing // positions)
        current = state_now.astype(jnp.float32)
        previous = shifted.astype(jnp.float32)
        mixed = mixed + weights[level_idx] * (c_high * current + s_high * previous)
        states.append(state_now)
        shifted_states.append(shifted)
        state_now = rounded(c_low * current + s_low * previous)
    top_state = state_now.astype(jnp.float32)
    mixed = mixed + weights[levels] * top_state
    activated = jax.nn.gelu(mixed).astype(jnp.bfloat16).reshape(-1, channels)
    projected = jnp.dot(activated, w_mix, preferred_element_type=jnp.float32)
    value_half = projected[:, :channels]
    gate_value = jax.nn.sigmoid(projected[:, channels:])
    upstream = received.reshape(-1, channels).astype(jnp.float32)
    grad_proj = jnp.concatenate(
        [upstream * gate_value, upstream * value_half * gate_value * (1.0 - gate_value)], axis=1
    ).astype(jnp.bfloat16)
    grad_act = jnp.einsum("rk,ck->rc", grad_proj, w_mix, preferred_element_type=jnp.float32)
    grad_weight = (
        lax.psum_scatter(
            jnp.einsum("rc,rk->ck", activated, grad_proj, preferred_element_type=jnp.float32),
            "seq",
            scatter_dimension=0,
            tiled=True,
        )
        * grad_scale
    )
    _, pullback = jax.vjp(jax.nn.gelu, mixed)
    grad_conv = pullback(grad_act.reshape(mixed.shape))[0]
    level_grads = [None] * (levels + 1)
    adjoint = weights[levels] * grad_conv
    level_grads[levels] = jnp.sum(grad_conv * top_state, axis=(0, 1))
    zero_row = jnp.zeros((channels,), jnp.float32)
    totals = (zero_row, zero_row, zero_row, zero_row)
    for level_idx in reversed(range(near_count, levels)):
        spacing = 2**level_idx
        current = states[level_idx].astype(jnp.float32)
        previous = shifted_states[level_idx].astype(jnp.float32)
        weighted = weights[level_idx] * grad_conv
        level_grads[level_idx] = jnp.sum(
            grad_conv * (c_high * current + s_high * previous), axis=(0, 1)
        )
        totals = tap_terms(totals, adjoint, weighted, current, previous)
        carried = rounded(s_low * adjoint + s_high * weighted)
        arrived = shifted_2(carried, "seq", -(spacing // positions)).astype(jnp.float32)
        adjoint = c_low * adjoint + c_high * weighted + arrived
    for level_idx in reversed(range(near_count)):
        spacing = 2**level_idx
        current = states[level_idx].astype(jnp.float32)
        previous = shifted_states[level_idx].astype(jnp.float32)
        weighted = weights[level_idx] * grad_conv
        level_grads[level_idx] = jnp.sum(
            grad_conv * (c_high * current + s_high * previous), axis=(0, 1)
        )
        totals = tap_terms(totals, adjoint, weighted, current, previous)
        carried = rounded(s_low * adjoint + s_high * weighted)
        rim_rows = shifted_2(carried[:, :spacing, :], "seq", -1)
        arrived = jnp.concatenate([carried[:, spacing:, :], rim_rows], axis=1).astype(jnp.float32)
        adjoint = c_low * adjoint + c_high * weighted + arrived
    angle_terms = jnp.stack(
        [c_low * totals[1] - s_low * totals[0], c_high * totals[3] - s_high * totals[2]]
    )
    angle_total, level_total = lax.psum((angle_terms, jnp.stack(level_grads)), "seq")
    grad_input = (received.astype(jnp.float32) + adjoint).astype(jnp.bfloat16)
    return (
        grad_input[None],
        (angle_total * grad_scale)[None],
        (level_total * grad_scale)[None],
        grad_weight[None],
    )


def solution(mesh):
    placed = (
        P("pipe", None, "seq", None),
        P("pipe", None, "seq", None),
        P("pipe", None, None),
        P("pipe", None, None),
        P("pipe", None, None),
    )
    return jax.shard_map(
        shards,
        mesh=mesh,
        in_specs=placed,
        out_specs=(
            P("pipe", None, "seq", None),
            P("pipe", None, None),
            P("pipe", None, None),
            P("pipe", "seq", None),
        ),
        check_vma=False,
    )
```

profile of v0, /device:TPU:0, one launch (start us, length us, event | category | flops | bytes accessed | tf_op | source)
XLA Modules:
  0.0 295.0 jit_solution(18199573209425934225)
XLA Ops:
  7.2 0.8 slice.196
  8.0 2.4 collective-permute-start.1
  10.3 1.0 slice_cosine_fusion
  11.4 1.5 fusion.14
  12.9 4.6 %collective-permute-start.2 = (bf16[2,2,1024]{2,1,0:T(2,128)(2,1)S(1)}, bf16[2,2,1024]{2,1,0:T(2,128)(2,1)S(1)}, u32[]{:S(2)}, u32[]{:S(2)}) collective-permute-start(bf16[2,2,1024]{2,1,0:T(2,128)(2,1)S(1)} %slice.198), channel_id=1, source_target_pairs={{0,1},{1,2},{2,3},{3,4},{4,5},{5,6},{6,7},{8,9},{9,10},{10,11},{11... | collective-permute-start | bytes 24584 | tf_op jit(solution)/shard_map/ppermute | solution.py:10
  17.5 0.8 collective-permute-done.2
  18.3 0.3 fusion.21
  18.6 3.9 %collective-permute-start.3 = (bf16[2,4,1024]{2,1,0:T(4,128)(2,1)S(1)}, bf16[2,4,1024]{2,1,0:T(4,128)(2,1)S(1)}, u32[]{:S(2)}, u32[]{:S(2)}) collective-permute-start(bf16[2,4,1024]{2,1,0:T(4,128)(2,1)S(1)} %slice.200), channel_id=1, source_target_pairs={{0,1},{1,2},{2,3},{3,4},{4,5},{5,6},{6,7},{8,9},{9,10},{10,11},{11... | collective-permute-start | bytes 49160 | tf_op jit(solution)/shard_map/ppermute | solution.py:10
  22.5 0.8 collective-permute-done.3
  23.3 0.3 fusion.28
  23.6 4.2 %collective-permute-start.4 = (bf16[2,8,1024]{2,1,0:T(8,128)(2,1)S(1)}, bf16[2,8,1024]{2,1,0:T(8,128)(2,1)S(1)}, u32[]{:S(2)}, u32[]{:S(2)}) collective-permute-start(bf16[2,8,1024]{2,1,0:T(8,128)(2,1)S(1)} %slice.202), channel_id=1, source_target_pairs={{0,1},{1,2},{2,3},{3,4},{4,5},{5,6},{6,7},{8,9},{9,10},{10,11},{11... | collective-permute-start | bytes 98312 | tf_op jit(solution)/shard_map/ppermute | solution.py:10
  27.9 0.8 collective-permute-done.4
  28.9 4.4 %collective-permute-start.5 = (bf16[2,16,1024]{2,1,0:T(8,128)(2,1)S(1)}, bf16[2,16,1024]{2,1,0:T(8,128)(2,1)S(1)}, u32[]{:S(2)}, u32[]{:S(2)}) collective-permute-start(bf16[2,16,1024]{2,1,0:T(8,128)(2,1)S(1)} %slice.204), channel_id=1, source_target_pairs={{0,1},{1,2},{2,3},{3,4},{4,5},{5,6},{6,7},{8,9},{9,10},{10,11},{11... | collective-permute-start | bytes 196616 | tf_op jit(solution)/shard_map/ppermute | solution.py:10
  33.3 0.8 collective-permute-done.5
  34.4 4.8 %collective-permute-start.6 = (bf16[2,32,1024]{2,1,0:T(8,128)(2,1)S(1)}, bf16[2,32,1024]{2,1,0:T(8,128)(2,1)S(1)}, u32[]{:S(2)}, u32[]{:S(2)}) collective-permute-start(bf16[2,32,1024]{2,1,0:T(8,128)(2,1)S(1)} %slice.206), channel_id=1, source_target_pairs={{0,1},{1,2},{2,3},{3,4},{4,5},{5,6},{6,7},{8,9},{9,10},{10,11},{11... | collective-permute-start | bytes 393224 | tf_op jit(solution)/shard_map/ppermute | solution.py:10
  39.3 0.9 collective-permute-done.6
  40.5 5.2 %collective-permute-start.7 = (bf16[2,64,1024]{2,1,0:T(8,128)(2,1)S(1)}, bf16[2,64,1024]{2,1,0:T(8,128)(2,1)S(1)}, u32[]{:S(2)}, u32[]{:S(2)}) collective-permute-start(bf16[2,64,1024]{2,1,0:T(8,128)(2,1)S(1)} %get-tuple-element.111), channel_id=1, source_target_pairs={{0,1},{1,2},{2,3},{3,4},{4,5},{5,6},{6,7},{8,9},{9,10},{10,11},{11... | collective-permute-start | bytes 786440 | tf_op jit(solution)/shard_map/ppermute | solution.py:10
  45.7 1.1 collective-permute-done.7
  47.1 6.5 %collective-permute-start.8 = (bf16[2,128,1024]{2,1,0:T(8,128)(2,1)S(1)}, bf16[2,128,1024]{2,1,0:T(8,128)(2,1)S(1)}, u32[]{:S(2)}, u32[]{:S(2)}) collective-permute-start(bf16[2,128,1024]{2,1,0:T(8,128)(2,1)S(1)} %fusion.56), channel_id=1, source_target_pairs={{0,1},{1,2},{2,3},{3,4},{4,5},{5,6},{6,7},{8,9},{9,10},{10,11},{11... | collective-permute-start | bytes 1572872 | tf_op jit(solution)/shard_map/ppermute | solution.py:10
  53.6 1.5 collective-permute-done.8
  55.3 11.4 %collective-permute-start.9 = (bf16[2,128,1024]{2,1,0:T(8,128)(2,1)S(1)}, bf16[2,128,1024]{2,1,0:T(8,128)(2,1)S(1)}, u32[]{:S(2)}, u32[]{:S(2)}) collective-permute-start(bf16[2,128,1024]{2,1,0:T(8,128)(2,1)S(1)} %fusion.63), channel_id=1, source_target_pairs={{0,2},{1,3},{2,4},{3,5},{4,6},{5,7},{8,10},{9,11},{10,12},{11,13},... | collective-permute-start | bytes 1572872 | tf_op jit(solution)/shard_map/ppermute | solution.py:10
  66.7 10.5 %collective-permute-done.9 = bf16[2,128,1024]{2,1,0:T(8,128)(2,1)S(1)} collective-permute-done((bf16[2,128,1024]{2,1,0:T(8,128)(2,1)S(1)}, bf16[2,128,1024]{2,1,0:T(8,128)(2,1)S(1)}, u32[]{:S(2)}, u32[]{:S(2)}) %collective-permute-start.9) | collective-permute-done | bytes 524320 | tf_op jit(solution)/shard_map/ppermute | solution.py:10
  77.5 5.4 %collective-permute-start.10 = (bf16[2,128,1024]{2,1,0:T(8,128)(2,1)S(1)}, bf16[2,128,1024]{2,1,0:T(8,128)(2,1)S(1)}, u32[]{:S(2)}, u32[]{:S(2)}) collective-permute-start(bf16[2,128,1024]{2,1,0:T(8,128)(2,1)S(1)} %fusion.70), channel_id=1, source_target_pairs={{0,4},{1,5},{2,6},{3,7},{8,12},{9,13},{10,14},{11,15},{16,20},{17,... | collective-permute-start | bytes 1572872 | tf_op jit(solution)/shard_map/ppermute | solution.py:10
  82.9 2.5 collective-permute-start
  85.5 7.0 %collective-permute-done.10 = bf16[2,128,1024]{2,1,0:T(8,128)(2,1)S(1)} collective-permute-done((bf16[2,128,1024]{2,1,0:T(8,128)(2,1)S(1)}, bf16[2,128,1024]{2,1,0:T(8,128)(2,1)S(1)}, u32[]{:S(2)}, u32[]{:S(2)}) %collective-permute-start.10) | collective-permute-done | bytes 524320 | tf_op jit(solution)/shard_map/ppermute | solution.py:10
  92.9 4.1 %multiply_convert_fusion = (bf16[2,128,1024]{2,1,0:T(8,128)(2,1)S(1)}, f32[2,128,1024]{2,1,0:T(8,128)}) fusion(bf16[2,128,1024]{2,1,0:T(8,128)(2,1)S(1)} %fusion.77, f32[1024]{0:T(1024)S(1)} %bitcast.171, bf16[2,128,1024]{2,1,0:T(8,128)(2,1)S(1)} %collective-permute-done.10, bf16[2,128,1024]{2,1,0:T(8,128)(2,1)S(1)} %fusion.70, f32[1024]{0:T(1024)S(1)} %bitcast.176, ...), kind=kLoop, calls=%fused_computation.216 | loop fusion | flops 26738688 | bytes 12636160 | tf_op jit(solution)/shard_map/convert_element_type | solution.py:75
  97.2 1.3 fusion.2
  98.5 0.6 fusion.97
  99.2 4.5 %fusion.91 = f32[1024,2048]{1,0:T(8,128)} fusion(bf16[256,1024]{1,0:T(8,128)(2,1)S(1)} %bitcast.104, bf16[256,1024]{1,0:T(8,128)(2,1)S(1)} %get-tuple-element.107, bf16[256,1024]{1,0:T(8,128)(2,1)S(1)} %get-tuple-element.106), kind=kOutput, calls=%fused_computation.177 | convolution fusion | flops 1075838976 | bytes 9961472 | tf_op jit(solution)/shard_map/rc,rk->ck/dot_general | solution.py:86
  103.9 5.0 %add_convert_fusion.9 = (bf16[2,128,1024]{2,1,0:T(8,128)(2,1)S(1)}, f32[2,128,1024]{2,1,0:T(8,128)S(1)}) fusion(f32[1024]{0:T(1024)} %bitcast.177, f32[1024]{0:T(1024)S(1)} %bitcast.135, f32[1024]{0:T(1024)S(1)} %bitcast.146, f32[1024]{0:T(1024)} %bitcast.172, f32[2,128,1024]{2,1,0:T(8,128)} %get-tuple-element.105, bf16[1,1024,2048]{2,1,0:T(8,128)(2,1)} %param.9, ...), kind=kOutput, calls=%fused_computation.215 | convolution fusion | flops 1082392576 | bytes 7880704 | tf_op jit(solution)/shard_map/rk,ck->rc/dot_general | solution.py:83
  108.9 1.3 collective-permute-start.11
  110.2 25.5 %collective-permute-done.11 = bf16[2,128,1024]{2,1,0:T(8,128)(2,1)S(1)} collective-permute-done((bf16[2,128,1024]{2,1,0:T(8,128)(2,1)S(1)}, bf16[2,128,1024]{2,1,0:T(8,128)(2,1)S(1)}, u32[]{:S(2)}, u32[]{:S(2)}) %collective-permute-start.11) | collective-permute-done | bytes 524320 | tf_op jit(solution)/shard_map/ppermute | solution.py:10
  135.7 0.4 add_convert_fusion.8
  136.2 1.6 collective-permute-start.12
  137.8 29.9 %collective-permute-done.12 = bf16[2,128,1024]{2,1,0:T(8,128)(2,1)S(1)} collective-permute-done((bf16[2,128,1024]{2,1,0:T(8,128)(2,1)S(1)}, bf16[2,128,1024]{2,1,0:T(8,128)(2,1)S(1)}, u32[]{:S(2)}, u32[]{:S(2)}) %collective-permute-start.12) | collective-permute-done | bytes 524320 | tf_op jit(solution)/shard_map/ppermute | solution.py:10
  167.7 3.2 %multiply_reduce_fusion = (f32[1024]{0:T(1024)}, f32[1024]{0:T(1024)}, f32[1024]{0:T(1024)}, f32[1024]{0:T(1024)}, f32[1024]{0:T(1024)}, /*index=5*/f32[1024]{0:...) fusion(f32[2,128,1024]{2,1,0:T(8,128)S(1)} %get-tuple-element.1, ...), kind=kLoop, calls=%fused_computation.187 | loop fusion | flops 17285120 | bytes 6389760 | tf_op jit(solution)/shard_map/reduce_sum | solution.py:105
  170.9 1.3 collective-permute-start.13
  172.1 2.5 collective-permute-done.13
  174.7 2.4 fusion.59
  177.4 1.3 collective-permute-start.14
  178.7 25.2 %collective-permute-done.14 = bf16[2,64,1024]{2,1,0:T(8,128)(2,1)S(1)} collective-permute-done((bf16[2,64,1024]{2,1,0:T(8,128)(2,1)S(1)}, bf16[2,64,1024]{2,1,0:T(8,128)(2,1)S(1)}, u32[]{:S(2)}, u32[]{:S(2)}) %collective-permute-start.14) | collective-permute-done | bytes 262176 | tf_op jit(solution)/shard_map/ppermute | solution.py:10
  203.9 1.1 fusion.52
  205.3 1.3 collective-permute-start.15
  206.7 13.9 %collective-permute-done.15 = bf16[2,32,1024]{2,1,0:T(8,128)(2,1)S(1)} collective-permute-done((bf16[2,32,1024]{2,1,0:T(8,128)(2,1)S(1)}, bf16[2,32,1024]{2,1,0:T(8,128)(2,1)S(1)}, u32[]{:S(2)}, u32[]{:S(2)}) %collective-permute-start.15) | collective-permute-done | bytes 131104 | tf_op jit(solution)/shard_map/ppermute | solution.py:10
  220.6 1.8 fusion.45
  222.7 1.3 collective-permute-start.16
  224.1 6.6 %collective-permute-done.16 = bf16[2,16,1024]{2,1,0:T(8,128)(2,1)S(1)} collective-permute-done((bf16[2,16,1024]{2,1,0:T(8,128)(2,1)S(1)}, bf16[2,16,1024]{2,1,0:T(8,128)(2,1)S(1)}, u32[]{:S(2)}, u32[]{:S(2)}) %collective-permute-start.16) | collective-permute-done | bytes 65568 | tf_op jit(solution)/shard_map/ppermute | solution.py:10
  230.7 0.5 fusion.38
  231.5 1.3 collective-permute-start.17
  232.8 4.2 %collective-permute-done.17 = bf16[2,8,1024]{2,1,0:T(8,128)(2,1)S(1)} collective-permute-done((bf16[2,8,1024]{2,1,0:T(8,128)(2,1)S(1)}, bf16[2,8,1024]{2,1,0:T(8,128)(2,1)S(1)}, u32[]{:S(2)}, u32[]{:S(2)}) %collective-permute-start.17) | collective-permute-done | bytes 32800 | tf_op jit(solution)/shard_map/ppermute | solution.py:10
  237.1 1.4 fusion.31
  238.7 1.3 collective-permute-start.18
  240.2 3.8 %collective-permute-done.18 = bf16[2,4,1024]{2,1,0:T(4,128)(2,1)S(1)} collective-permute-done((bf16[2,4,1024]{2,1,0:T(4,128)(2,1)S(1)}, bf16[2,4,1024]{2,1,0:T(4,128)(2,1)S(1)}, u32[]{:S(2)}, u32[]{:S(2)}) %collective-permute-start.18) | collective-permute-done | bytes 16416 | tf_op jit(solution)/shard_map/ppermute | solution.py:10
  243.9 0.6 fusion.24
  245.1 1.3 collective-permute-start.19
  246.6 3.6 %collective-permute-done.19 = bf16[2,2,1024]{2,1,0:T(2,128)(2,1)S(1)} collective-permute-done((bf16[2,2,1024]{2,1,0:T(2,128)(2,1)S(1)}, bf16[2,2,1024]{2,1,0:T(2,128)(2,1)S(1)}, u32[]{:S(2)}, u32[]{:S(2)}) %collective-permute-start.19) | collective-permute-done | bytes 8224 | tf_op jit(solution)/shard_map/ppermute | solution.py:10
  250.2 0.9 fusion.17
  251.3 1.3 collective-permute-start.20
  253.2 0.3 fusion.104
  253.4 29.8 %all-reduce = (f32[2,1024]{1,0:T(2,128)S(1)}, f32[11,1024]{1,0:T(8,128)S(1)}) all-reduce(f32[2,1024]{1,0:T(2,128)S(1)} %pad_maximum_fusion.7, f32[11,1024]{1,0:T(8,128)S(1)} %stack.53), channel_id=1, replica_groups=mesh['pipe'=4,'seq'=8] {'seq'}, use_global_device_ids=true, to_apply=%region_40.0 | all-reduce | flops 13312 | bytes 106496 | tf_op jit(solution)/shard_map/psum | solution.py:128
  283.3 0.6 multiply_bitcast_fusion.1
  284.0 0.7 broadcast_in_dim.10
  284.7 1.2 fusion.102
  285.9 2.3 multiply_bitcast_fusion
  (260 shorter events, 4.7 us)
Async XLA Ops:
  7.2 278.7 %reduce-scatter.2.cloned.1.call-start = ((), (), s32[]{:S(2)}) async-start(), calls=%async_computation.1 | async-start | bytes 9437184 | tf_op jit(solution)/shard_map/reduce_scatter | solution.py:85
  8.0 3.4 %collective-permute-start.1 = (bf16[2,1,1024]{2,1,0:T(2,128)(2,1)S(1)}, bf16[2,1,1024]{2,1,0:T(2,128)(2,1)S(1)}, u32[]{:S(2)}, u32[]{:S(2)}) collective-permute-start(bf16[2,1,1024]{2,1,0:T(2,128)(2,1)S(1)} %slice.196), channel_id=1, source_target_pairs={{0,1},{1,2},{2,3},{3,4},{4,5},{5,6},{6,7},{8,9},{9,10},{10,11},{11... | collective-permute-start | bytes 12296 | tf_op jit(solution)/shard_map/ppermute | solution.py:10
  11.4 81.4 %copy-start.63 = (bf16[2,1,1024]{2,1,0:T(2,128)(2,1)}, bf16[2,1,1024]{2,1,0:T(2,128)(2,1)S(1)}, u32[]{:S(2)}) copy-start(bf16[2,1,1024]{2,1,0:T(2,128)(2,1)S(1)} %collective-permute-done.1) | copy-start | bytes 12292
  12.9 5.4 %collective-permute-start.2 = (bf16[2,2,1024]{2,1,0:T(2,128)(2,1)S(1)}, bf16[2,2,1024]{2,1,0:T(2,128)(2,1)S(1)}, u32[]{:S(2)}, u32[]{:S(2)}) collective-permute-start(bf16[2,2,1024]{2,1,0:T(2,128)(2,1)S(1)} %slice.198), channel_id=1, source_target_pairs={{0,1},{1,2},{2,3},{3,4},{4,5},{5,6},{6,7},{8,9},{9,10},{10,11},{11... | collective-permute-start | bytes 24584 | tf_op jit(solution)/shard_map/ppermute | solution.py:10
  18.3 74.5 %copy-start.41 = (bf16[2,2,1024]{2,1,0:T(2,128)(2,1)}, bf16[2,2,1024]{2,1,0:T(2,128)(2,1)S(1)}, u32[]{:S(2)}) copy-start(bf16[2,2,1024]{2,1,0:T(2,128)(2,1)S(1)} %collective-permute-done.2) | copy-start | bytes 24580
  18.6 4.7 %collective-permute-start.3 = (bf16[2,4,1024]{2,1,0:T(4,128)(2,1)S(1)}, bf16[2,4,1024]{2,1,0:T(4,128)(2,1)S(1)}, u32[]{:S(2)}, u32[]{:S(2)}) collective-permute-start(bf16[2,4,1024]{2,1,0:T(4,128)(2,1)S(1)} %slice.200), channel_id=1, source_target_pairs={{0,1},{1,2},{2,3},{3,4},{4,5},{5,6},{6,7},{8,9},{9,10},{10,11},{11... | collective-permute-start | bytes 49160 | tf_op jit(solution)/shard_map/ppermute | solution.py:10
  23.3 69.5 %copy-start.39 = (bf16[2,4,1024]{2,1,0:T(4,128)(2,1)}, bf16[2,4,1024]{2,1,0:T(4,128)(2,1)S(1)}, u32[]{:S(2)}) copy-start(bf16[2,4,1024]{2,1,0:T(4,128)(2,1)S(1)} %collective-permute-done.3) | copy-start | bytes 49156
  23.6 5.1 %collective-permute-start.4 = (bf16[2,8,1024]{2,1,0:T(8,128)(2,1)S(1)}, bf16[2,8,1024]{2,1,0:T(8,128)(2,1)S(1)}, u32[]{:S(2)}, u32[]{:S(2)}) collective-permute-start(bf16[2,8,1024]{2,1,0:T(8,128)(2,1)S(1)} %slice.202), channel_id=1, source_target_pairs={{0,1},{1,2},{2,3},{3,4},{4,5},{5,6},{6,7},{8,9},{9,10},{10,11},{11... | collective-permute-start | bytes 98312 | tf_op jit(solution)/shard_map/ppermute | solution.py:10
  27.9 64.9 %copy-start.7 = (bf16[2,120,1024]{2,1,0:T(8,128)(2,1)}, bf16[2,120,1024]{2,1,0:T(8,128)(2,1)S(1)}, u32[]{:S(2)}) copy-start(bf16[2,120,1024]{2,1,0:T(8,128)(2,1)S(1)} %slice.203) | copy-start | bytes 1474564
  28.7 64.1 %copy-start.37 = (bf16[2,8,1024]{2,1,0:T(8,128)(2,1)}, bf16[2,8,1024]{2,1,0:T(8,128)(2,1)S(1)}, u32[]{:S(2)}) copy-start(bf16[2,8,1024]{2,1,0:T(8,128)(2,1)S(1)} %collective-permute-done.4) | copy-start | bytes 98308
  28.9 63.9 %copy-start.3 = (bf16[2,128,1024]{2,1,0:T(8,128)(2,1)}, bf16[2,128,1024]{2,1,0:T(8,128)(2,1)S(1)}, u32[]{:S(2)}) copy-start(bf16[2,128,1024]{2,1,0:T(8,128)(2,1)S(1)} %fusion.35) | copy-start | bytes 1572868
  28.9 5.3 %collective-permute-start.5 = (bf16[2,16,1024]{2,1,0:T(8,128)(2,1)S(1)}, bf16[2,16,1024]{2,1,0:T(8,128)(2,1)S(1)}, u32[]{:S(2)}, u32[]{:S(2)}) collective-permute-start(bf16[2,16,1024]{2,1,0:T(8,128)(2,1)S(1)} %slice.204), channel_id=1, source_target_pairs={{0,1},{1,2},{2,3},{3,4},{4,5},{5,6},{6,7},{8,9},{9,10},{10,11},{11... | collective-permute-start | bytes 196616 | tf_op jit(solution)/shard_map/ppermute | solution.py:10
  33.3 59.5 %copy-start.15 = (bf16[2,112,1024]{2,1,0:T(8,128)(2,1)}, bf16[2,112,1024]{2,1,0:T(8,128)(2,1)S(1)}, u32[]{:S(2)}) copy-start(bf16[2,112,1024]{2,1,0:T(8,128)(2,1)S(1)} %slice.205) | copy-start | bytes 1376260
  34.2 58.7 %copy-start.35 = (bf16[2,16,1024]{2,1,0:T(8,128)(2,1)}, bf16[2,16,1024]{2,1,0:T(8,128)(2,1)S(1)}, u32[]{:S(2)}) copy-start(bf16[2,16,1024]{2,1,0:T(8,128)(2,1)S(1)} %collective-permute-done.5) | copy-start | bytes 196612
  34.4 58.5 %copy-start.1 = (bf16[2,128,1024]{2,1,0:T(8,128)(2,1)}, bf16[2,128,1024]{2,1,0:T(8,128)(2,1)S(1)}, u32[]{:S(2)}) copy-start(bf16[2,128,1024]{2,1,0:T(8,128)(2,1)S(1)} %fusion.42) | copy-start | bytes 1572868
  34.4 48.5 %copy-start.104 = (bf16[1,2,128,1024]{3,2,1,0:T(8,128)(2,1)S(1)}, bf16[1,2,128,1024]{3,2,1,0:T(8,128)(2,1)}, u32[]{:S(2)}) copy-start(bf16[1,2,128,1024]{3,2,1,0:T(8,128)(2,1)} %param.6) | copy-start | bytes 1572868
  34.4 51.0 %copy-start.67 = (f32[1,11,1024]{2,0,1:T(1,128)S(1)}, f32[1,11,1024]{2,0,1:T(1,128)}, u32[]{:S(2)}) copy-start(f32[1,11,1024]{2,0,1:T(1,128)} %param.8) | copy-start | bytes 135172
  34.4 5.8 %collective-permute-start.6 = (bf16[2,32,1024]{2,1,0:T(8,128)(2,1)S(1)}, bf16[2,32,1024]{2,1,0:T(8,128)(2,1)S(1)}, u32[]{:S(2)}, u32[]{:S(2)}) collective-permute-start(bf16[2,32,1024]{2,1,0:T(8,128)(2,1)S(1)} %slice.206), channel_id=1, source_target_pairs={{0,1},{1,2},{2,3},{3,4},{4,5},{5,6},{6,7},{8,9},{9,10},{10,11},{11... | collective-permute-start | bytes 393224 | tf_op jit(solution)/shard_map/ppermute | solution.py:10
  39.3 53.6 %copy-start = (bf16[1,2,128,1024]{3,2,1,0:T(8,128)(2,1)S(1)}, bf16[1,2,128,1024]{3,2,1,0:T(8,128)(2,1)}, u32[]{:S(2)}) copy-start(bf16[1,2,128,1024]{3,2,1,0:T(8,128)(2,1)} %param.5) | copy-start | bytes 1572868
  40.2 52.7 %copy-start.29 = (bf16[2,32,1024]{2,1,0:T(8,128)(2,1)}, bf16[2,32,1024]{2,1,0:T(8,128)(2,1)S(1)}, u32[]{:S(2)}) copy-start(bf16[2,32,1024]{2,1,0:T(8,128)(2,1)S(1)} %collective-permute-done.6) | copy-start | bytes 393220
  40.4 56.6 %copy-start.5 = (bf16[2,128,1024]{2,1,0:T(8,128)(2,1)}, bf16[2,128,1024]{2,1,0:T(8,128)(2,1)S(1)}, u32[]{:S(2)}) copy-start(bf16[2,128,1024]{2,1,0:T(8,128)(2,1)S(1)} %fusion.49) | copy-start | bytes 1572868
  40.5 56.5 %copy-start.25 = (bf16[2,64,1024]{2,1,0:T(8,128)(2,1)}, bf16[2,64,1024]{2,1,0:T(8,128)(2,1)S(1)}, u32[]{:S(2)}) copy-start(bf16[2,64,1024]{2,1,0:T(8,128)(2,1)S(1)} %get-tuple-element.112) | copy-start | bytes 786436
  40.5 6.4 %collective-permute-start.7 = (bf16[2,64,1024]{2,1,0:T(8,128)(2,1)S(1)}, bf16[2,64,1024]{2,1,0:T(8,128)(2,1)S(1)}, u32[]{:S(2)}, u32[]{:S(2)}) collective-permute-start(bf16[2,64,1024]{2,1,0:T(8,128)(2,1)S(1)} %get-tuple-element.111), channel_id=1, source_target_pairs={{0,1},{1,2},{2,3},{3,4},{4,5},{5,6},{6,7},{8,9},{9,10},{10,11},{11... | collective-permute-start | bytes 786440 | tf_op jit(solution)/shard_map/ppermute | solution.py:10
  46.8 50.1 %copy-start.27 = (bf16[2,64,1024]{2,1,0:T(8,128)(2,1)}, bf16[2,64,1024]{2,1,0:T(8,128)(2,1)S(1)}, u32[]{:S(2)}) copy-start(bf16[2,64,1024]{2,1,0:T(8,128)(2,1)S(1)} %collective-permute-done.7) | copy-start | bytes 786436
  47.1 49.9 %copy-start.9 = (bf16[2,128,1024]{2,1,0:T(8,128)(2,1)}, bf16[2,128,1024]{2,1,0:T(8,128)(2,1)S(1)}, u32[]{:S(2)}) copy-start(bf16[2,128,1024]{2,1,0:T(8,128)(2,1)S(1)} %fusion.56) | copy-start | bytes 1572868
  47.1 8.0 %collective-permute-start.8 = (bf16[2,128,1024]{2,1,0:T(8,128)(2,1)S(1)}, bf16[2,128,1024]{2,1,0:T(8,128)(2,1)S(1)}, u32[]{:S(2)}, u32[]{:S(2)}) collective-permute-start(bf16[2,128,1024]{2,1,0:T(8,128)(2,1)S(1)} %fusion.56), channel_id=1, source_target_pairs={{0,1},{1,2},{2,3},{3,4},{4,5},{5,6},{6,7},{8,9},{9,10},{10,11},{11... | collective-permute-start | bytes 1572872 | tf_op jit(solution)/shard_map/ppermute | solution.py:10
  55.1 41.9 %copy-start.17 = (bf16[2,128,1024]{2,1,0:T(8,128)(2,1)}, bf16[2,128,1024]{2,1,0:T(8,128)(2,1)S(1)}, u32[]{:S(2)}) copy-start(bf16[2,128,1024]{2,1,0:T(8,128)(2,1)S(1)} %collective-permute-done.8) | copy-start | bytes 1572868
  55.3 41.7 %copy-start.11 = (bf16[2,128,1024]{2,1,0:T(8,128)(2,1)}, bf16[2,128,1024]{2,1,0:T(8,128)(2,1)S(1)}, u32[]{:S(2)}) copy-start(bf16[2,128,1024]{2,1,0:T(8,128)(2,1)S(1)} %fusion.63) | copy-start | bytes 1572868
  55.3 21.9 %collective-permute-start.9 = (bf16[2,128,1024]{2,1,0:T(8,128)(2,1)S(1)}, bf16[2,128,1024]{2,1,0:T(8,128)(2,1)S(1)}, u32[]{:S(2)}, u32[]{:S(2)}) collective-permute-start(bf16[2,128,1024]{2,1,0:T(8,128)(2,1)S(1)} %fusion.63), channel_id=1, source_target_pairs={{0,2},{1,3},{2,4},{3,5},{4,6},{5,7},{8,10},{9,11},{10,12},{11,13},... | collective-permute-start | bytes 1572872 | tf_op jit(solution)/shard_map/ppermute | solution.py:10
  77.2 19.8 %copy-start.19 = (bf16[2,128,1024]{2,1,0:T(8,128)(2,1)}, bf16[2,128,1024]{2,1,0:T(8,128)(2,1)S(1)}, u32[]{:S(2)}) copy-start(bf16[2,128,1024]{2,1,0:T(8,128)(2,1)S(1)} %collective-permute-done.9) | copy-start | bytes 1572868
  77.4 19.6 %copy-start.13 = (bf16[2,128,1024]{2,1,0:T(8,128)(2,1)}, bf16[2,128,1024]{2,1,0:T(8,128)(2,1)S(1)}, u32[]{:S(2)}) copy-start(bf16[2,128,1024]{2,1,0:T(8,128)(2,1)S(1)} %fusion.70) | copy-start | bytes 1572868
  77.5 15.1 %collective-permute-start.10 = (bf16[2,128,1024]{2,1,0:T(8,128)(2,1)S(1)}, bf16[2,128,1024]{2,1,0:T(8,128)(2,1)S(1)}, u32[]{:S(2)}, u32[]{:S(2)}) collective-permute-start(bf16[2,128,1024]{2,1,0:T(8,128)(2,1)S(1)} %fusion.70), channel_id=1, source_target_pairs={{0,4},{1,5},{2,6},{3,7},{8,12},{9,13},{10,14},{11,15},{16,20},{17,... | collective-permute-start | bytes 1572872 | tf_op jit(solution)/shard_map/ppermute | solution.py:10
  82.9 15.5 %collective-permute-start = (bf16[1,2,128,1024]{3,2,1,0:T(8,128)(2,1)S(1)}, bf16[1,2,128,1024]{3,2,1,0:T(8,128)(2,1)S(1)}, u32[]{:S(2)}, u32[]{:S(2)}) collective-permute-start(bf16[1,2,128,1024]{3,2,1,0:T(8,128)(2,1)S(1)} %copy-done.104), channel_id=1, source_target_pairs={{0,24},{8,0},{16,8},{24,16},{1,25},{9,1},{17,9},{25,17},{2,26},{10... | collective-permute-start | bytes 1572872 | tf_op jit(solution)/shard_map/ppermute | solution.py:16
  103.8 31.9 %copy-start.44 = (f32[1,1,1024]{2,0,1:T(1,128)S(1)}, f32[1,1,1024]{2,0,1:T(1,128)}, u32[]{:S(2)}) copy-start(f32[1,1,1024]{2,0,1:T(1,128)} %copy-done.43) | copy-start | bytes 12292
  103.8 31.9 %copy-start.46 = (f32[1,1,1024]{2,0,1:T(1,128)S(1)}, f32[1,1,1024]{2,0,1:T(1,128)}, u32[]{:S(2)}) copy-start(f32[1,1,1024]{2,0,1:T(1,128)} %copy-done.45) | copy-start | bytes 12292
  103.8 31.8 %copy-start.48 = (f32[1,1,1024]{2,0,1:T(1,128)S(1)}, f32[1,1,1024]{2,0,1:T(1,128)}, u32[]{:S(2)}) copy-start(f32[1,1,1024]{2,0,1:T(1,128)} %copy-done.47) | copy-start | bytes 12292
  103.8 63.8 %copy-start.10 = (bf16[2,128,1024]{2,1,0:T(8,128)(2,1)S(1)}, bf16[2,128,1024]{2,1,0:T(8,128)(2,1)}, u32[]{:S(2)}) copy-start(bf16[2,128,1024]{2,1,0:T(8,128)(2,1)} %copy-done.9) | copy-start | bytes 1572868
  103.8 63.8 %copy-start.12 = (bf16[2,128,1024]{2,1,0:T(8,128)(2,1)S(1)}, bf16[2,128,1024]{2,1,0:T(8,128)(2,1)}, u32[]{:S(2)}) copy-start(bf16[2,128,1024]{2,1,0:T(8,128)(2,1)} %copy-done.11) | copy-start | bytes 1572868
  103.9 63.8 %copy-start.14 = (bf16[2,128,1024]{2,1,0:T(8,128)(2,1)S(1)}, bf16[2,128,1024]{2,1,0:T(8,128)(2,1)}, u32[]{:S(2)}) copy-start(bf16[2,128,1024]{2,1,0:T(8,128)(2,1)} %copy-done.13) | copy-start | bytes 1572868
  103.9 63.8 %copy-start.18 = (bf16[2,128,1024]{2,1,0:T(8,128)(2,1)S(1)}, bf16[2,128,1024]{2,1,0:T(8,128)(2,1)}, u32[]{:S(2)}) copy-start(bf16[2,128,1024]{2,1,0:T(8,128)(2,1)} %copy-done.17) | copy-start | bytes 1572868
  103.9 63.8 %copy-start.20 = (bf16[2,128,1024]{2,1,0:T(8,128)(2,1)S(1)}, bf16[2,128,1024]{2,1,0:T(8,128)(2,1)}, u32[]{:S(2)}) copy-start(bf16[2,128,1024]{2,1,0:T(8,128)(2,1)} %copy-done.19) | copy-start | bytes 1572868
  103.9 63.8 %copy-start.22 = (bf16[2,128,1024]{2,1,0:T(8,128)(2,1)S(1)}, bf16[2,128,1024]{2,1,0:T(8,128)(2,1)}, u32[]{:S(2)}) copy-start(bf16[2,128,1024]{2,1,0:T(8,128)(2,1)} %copy-done.21) | copy-start | bytes 1572868
  103.9 63.8 %copy-start.24 = (bf16[2,128,1024]{2,1,0:T(8,128)(2,1)S(1)}, bf16[2,128,1024]{2,1,0:T(8,128)(2,1)}, u32[]{:S(2)}) copy-start(bf16[2,128,1024]{2,1,0:T(8,128)(2,1)} %copy-done.23) | copy-start | bytes 1572868
  103.9 63.8 %copy-start.66 = (f32[1,1,1024]{2,0,1:T(1,128)S(1)}, f32[1,1,1024]{2,0,1:T(1,128)}, u32[]{:S(2)}) copy-start(f32[1,1,1024]{2,0,1:T(1,128)} %copy-done.65) | copy-start | bytes 12292
  108.9 26.8 %collective-permute-start.11 = (bf16[2,128,1024]{2,1,0:T(8,128)(2,1)S(1)}, bf16[2,128,1024]{2,1,0:T(8,128)(2,1)S(1)}, u32[]{:S(2)}, u32[]{:S(2)}) collective-permute-start(bf16[2,128,1024]{2,1,0:T(8,128)(2,1)S(1)} %get-tuple-element.130), channel_id=1, source_target_pairs={{4,0},{5,1},{6,2},{7,3},{12,8},{13,9},{14,10},{15,11},{20,16},{21,... | collective-permute-start | bytes 1572872 | tf_op jit(solution)/shard_map/ppermute | solution.py:10
  135.7 39.0 %copy-start.2 = (bf16[2,128,1024]{2,1,0:T(8,128)(2,1)S(1)}, bf16[2,128,1024]{2,1,0:T(8,128)(2,1)}, u32[]{:S(2)}) copy-start(bf16[2,128,1024]{2,1,0:T(8,128)(2,1)} %copy-done.1) | copy-start | bytes 1572868
  135.7 39.0 %copy-start.6 = (bf16[2,128,1024]{2,1,0:T(8,128)(2,1)S(1)}, bf16[2,128,1024]{2,1,0:T(8,128)(2,1)}, u32[]{:S(2)}) copy-start(bf16[2,128,1024]{2,1,0:T(8,128)(2,1)} %copy-done.5) | copy-start | bytes 1572868
  135.7 39.0 %copy-start.26 = (bf16[2,64,1024]{2,1,0:T(8,128)(2,1)S(1)}, bf16[2,64,1024]{2,1,0:T(8,128)(2,1)}, u32[]{:S(2)}) copy-start(bf16[2,64,1024]{2,1,0:T(8,128)(2,1)} %copy-done.25) | copy-start | bytes 786436
  135.7 39.0 %copy-start.28 = (bf16[2,64,1024]{2,1,0:T(8,128)(2,1)S(1)}, bf16[2,64,1024]{2,1,0:T(8,128)(2,1)}, u32[]{:S(2)}) copy-start(bf16[2,64,1024]{2,1,0:T(8,128)(2,1)} %copy-done.27) | copy-start | bytes 786436
  135.7 39.0 %copy-start.30 = (bf16[2,32,1024]{2,1,0:T(8,128)(2,1)S(1)}, bf16[2,32,1024]{2,1,0:T(8,128)(2,1)}, u32[]{:S(2)}) copy-start(bf16[2,32,1024]{2,1,0:T(8,128)(2,1)} %copy-done.29) | copy-start | bytes 393220
  135.7 39.0 %copy-start.54 = (f32[1,1,1024]{2,0,1:T(1,128)S(1)}, f32[1,1,1024]{2,0,1:T(1,128)}, u32[]{:S(2)}) copy-start(f32[1,1,1024]{2,0,1:T(1,128)} %copy-done.53) | copy-start | bytes 12292
  135.7 39.0 %copy-start.56 = (f32[1,1,1024]{2,0,1:T(1,128)S(1)}, f32[1,1,1024]{2,0,1:T(1,128)}, u32[]{:S(2)}) copy-start(f32[1,1,1024]{2,0,1:T(1,128)} %copy-done.55) | copy-start | bytes 12292
  136.2 31.5 %collective-permute-start.12 = (bf16[2,128,1024]{2,1,0:T(8,128)(2,1)S(1)}, bf16[2,128,1024]{2,1,0:T(8,128)(2,1)S(1)}, u32[]{:S(2)}, u32[]{:S(2)}) collective-permute-start(bf16[2,128,1024]{2,1,0:T(8,128)(2,1)S(1)} %add_convert_fusion.8), channel_id=1, source_target_pairs={{2,0},{3,1},{4,2},{5,3},{6,4},{7,5},{10,8},{11,9},{12,10},{13,11},... | collective-permute-start | bytes 1572872 | tf_op jit(solution)/shard_map/ppermute | solution.py:10
  170.9 3.8 %collective-permute-start.13 = (bf16[2,128,1024]{2,1,0:T(8,128)(2,1)S(1)}, bf16[2,128,1024]{2,1,0:T(8,128)(2,1)S(1)}, u32[]{:S(2)}, u32[]{:S(2)}) collective-permute-start(bf16[2,128,1024]{2,1,0:T(8,128)(2,1)S(1)} %get-tuple-element.108), channel_id=1, source_target_pairs={{1,0},{2,1},{3,2},{4,3},{5,4},{6,5},{7,6},{9,8},{10,9},{11,10},{12... | collective-permute-start | bytes 1572872 | tf_op jit(solution)/shard_map/ppermute | solution.py:10
  177.4 26.5 %collective-permute-start.14 = (bf16[2,64,1024]{2,1,0:T(8,128)(2,1)S(1)}, bf16[2,64,1024]{2,1,0:T(8,128)(2,1)S(1)}, u32[]{:S(2)}, u32[]{:S(2)}) collective-permute-start(bf16[2,64,1024]{2,1,0:T(8,128)(2,1)S(1)} %get-tuple-element.110), channel_id=1, source_target_pairs={{1,0},{2,1},{3,2},{4,3},{5,4},{6,5},{7,6},{9,8},{10,9},{11,10},{12... | collective-permute-start | bytes 786440 | tf_op jit(solution)/shard_map/ppermute | solution.py:10
  203.9 16.7 %copy-start.38 = (bf16[2,8,1024]{2,1,0:T(8,128)(2,1)S(1)}, bf16[2,8,1024]{2,1,0:T(8,128)(2,1)}, u32[]{:S(2)}) copy-start(bf16[2,8,1024]{2,1,0:T(8,128)(2,1)} %copy-done.37) | copy-start | bytes 98308
  203.9 16.7 %copy-start.60 = (f32[1,1,1024]{2,0,1:T(1,128)S(1)}, f32[1,1,1024]{2,0,1:T(1,128)}, u32[]{:S(2)}) copy-start(f32[1,1,1024]{2,0,1:T(1,128)} %copy-done.59) | copy-start | bytes 12292
  205.3 15.2 %collective-permute-start.15 = (bf16[2,32,1024]{2,1,0:T(8,128)(2,1)S(1)}, bf16[2,32,1024]{2,1,0:T(8,128)(2,1)S(1)}, u32[]{:S(2)}, u32[]{:S(2)}) collective-permute-start(bf16[2,32,1024]{2,1,0:T(8,128)(2,1)S(1)} %slice.215), channel_id=1, source_target_pairs={{1,0},{2,1},{3,2},{4,3},{5,4},{6,5},{7,6},{9,8},{10,9},{11,10},{12... | collective-permute-start | bytes 393224 | tf_op jit(solution)/shard_map/ppermute | solution.py:10
  222.7 8.0 %collective-permute-start.16 = (bf16[2,16,1024]{2,1,0:T(8,128)(2,1)S(1)}, bf16[2,16,1024]{2,1,0:T(8,128)(2,1)S(1)}, u32[]{:S(2)}, u32[]{:S(2)}) collective-permute-start(bf16[2,16,1024]{2,1,0:T(8,128)(2,1)S(1)} %slice.217), channel_id=1, source_target_pairs={{1,0},{2,1},{3,2},{4,3},{5,4},{6,5},{7,6},{9,8},{10,9},{11,10},{12... | collective-permute-start | bytes 196616 | tf_op jit(solution)/shard_map/ppermute | solution.py:10
  231.5 5.6 %collective-permute-start.17 = (bf16[2,8,1024]{2,1,0:T(8,128)(2,1)S(1)}, bf16[2,8,1024]{2,1,0:T(8,128)(2,1)S(1)}, u32[]{:S(2)}, u32[]{:S(2)}) collective-permute-start(bf16[2,8,1024]{2,1,0:T(8,128)(2,1)S(1)} %slice.219), channel_id=1, source_target_pairs={{1,0},{2,1},{3,2},{4,3},{5,4},{6,5},{7,6},{9,8},{10,9},{11,10},{12... | collective-permute-start | bytes 98312 | tf_op jit(solution)/shard_map/ppermute | solution.py:10
  238.7 5.2 %collective-permute-start.18 = (bf16[2,4,1024]{2,1,0:T(4,128)(2,1)S(1)}, bf16[2,4,1024]{2,1,0:T(4,128)(2,1)S(1)}, u32[]{:S(2)}, u32[]{:S(2)}) collective-permute-start(bf16[2,4,1024]{2,1,0:T(4,128)(2,1)S(1)} %slice.221), channel_id=1, source_target_pairs={{1,0},{2,1},{3,2},{4,3},{5,4},{6,5},{7,6},{9,8},{10,9},{11,10},{12... | collective-permute-start | bytes 49160 | tf_op jit(solution)/shard_map/ppermute | solution.py:10
  245.1 5.0 %collective-permute-start.19 = (bf16[2,2,1024]{2,1,0:T(2,128)(2,1)S(1)}, bf16[2,2,1024]{2,1,0:T(2,128)(2,1)S(1)}, u32[]{:S(2)}, u32[]{:S(2)}) collective-permute-start(bf16[2,2,1024]{2,1,0:T(2,128)(2,1)S(1)} %slice.223), channel_id=1, source_target_pairs={{1,0},{2,1},{3,2},{4,3},{5,4},{6,5},{7,6},{9,8},{10,9},{11,10},{12... | collective-permute-start | bytes 24584 | tf_op jit(solution)/shard_map/ppermute | solution.py:10
  246.6 38.1 %copy-start.34 = (bf16[1,2,128,1024]{3,2,1,0:T(8,128)(2,1)S(1)}, bf16[1,2,128,1024]{3,2,1,0:T(8,128)(2,1)}, u32[]{:S(2)}) copy-start(bf16[1,2,128,1024]{3,2,1,0:T(8,128)(2,1)} %copy-done.33) | copy-start | bytes 1572868
  251.3 33.3 %collective-permute-start.20 = (bf16[2,1,1024]{2,1,0:T(2,128)(2,1)S(1)}, bf16[2,1,1024]{2,1,0:T(2,128)(2,1)S(1)}, u32[]{:S(2)}, u32[]{:S(2)}) collective-permute-start(bf16[2,1,1024]{2,1,0:T(2,128)(2,1)S(1)} %slice.225), channel_id=1, source_target_pairs={{1,0},{2,1},{3,2},{4,3},{5,4},{6,5},{7,6},{9,8},{10,9},{11,10},{12... | collective-permute-start | bytes 12296 | tf_op jit(solution)/shard_map/ppermute | solution.py:10
  (63 other events, 585.5 us)
Sparse Core Ops, SparseCore 0:
  103.9 130.6 reduce-scatter.1
where the time goes:
time: 296 us; the launch traced here: 295 us
  waiting for transfers between devices  139 us (47%)
  starting transfers between devices  68.5 us (23%)
  blocking collectives  29.8 us (10%)
  other arithmetic  26.6 us (9%)
  between operations  15.9 us (5%)
  matrix products  10.7 us (4%)
  local copies, waits for them, and re-layouts  3.87 us (1%)
    ppermute x20, waiting for transfers between devices, shifted_2(): return lax.ppermute(block, axis, route)  139 us
    ppermute x20, starting transfers between devices, shifted_2(): return lax.ppermute(block, axis, route)  66 us
    psum x1, blocking collectives, shards(): lax.psum((angle_terms, jnp.stack(level_grads)), 'seq')  29.8 us
    reduce_sum x7, other arithmetic, tap_terms(): jnp.sum(adjoint * previous, axis=(0, 1))  8.78 us
  transfers between devices with their start and end apart: 22, of which 18 were waited for; matrix products, arithmetic and copies ran while one was open for 10% of the time, Pallas kernels for 0%

commit v1 on v0

--- a/solution.py
+++ b/solution.py
@@ -1,6 +1,10 @@
+import functools
+
 import jax
 import jax.numpy as jnp
 from jax import lax
+from jax.experimental import pallas as pl
+from jax.experimental.pallas import tpu as pltpu
 from jax.sharding import PartitionSpec as P
 
 
@@ -34,7 +38,7 @@
     )
 
 
-def shards(inputs, incoming, angles, level_weights, mix_weight):
+def shards_by_levels(inputs, incoming, angles, level_weights, mix_weight):
     activations = inputs[0]
     sequences, positions, channels = activations.shape
     seq_devices = lax.axis_size("seq")
@@ -135,7 +139,439 @@
     )
 
 
+MESH = pl.DeviceIdType.MESH
+CORES = 2
+F32 = jnp.float32
+BF16 = jnp.bfloat16
+
+
+def whole_kernel(
+    pipes, n, levels,
+    x_ref, inc_ref, ang_ref, lw_ref, w_hbm,
+    gin_ref, small_ref, gmix_ref,
+    xin, cot, wv, actc, actf, gp, ga, gab, gac, dgelu, adjs, adjf, coef, accs, mine,
+    pb, px, txr, rxr, txl, rxl, states, adjoints,
+    w_sem, cot_s, cot_r, loc_sem, a_s, a_r, px_s, px_r, rs_s, rs_r,
+):
+    batch, rows, chans = inc_ref.shape
+    seq = n * rows
+    slab = chans // n
+    nz = n // CORES
+    me = lax.axis_index("seq")
+    pipe = lax.axis_index("pipe")
+    z = me // CORES
+    core = me % CORES
+    my_slab = pl.ds(pl.multiple_of(me * slab, slab), slab)
+    my_rows = pl.ds(pl.multiple_of(me * rows, rows), rows)
+
+    def times(d, size):
+        return d * size if isinstance(d, int) else pl.multiple_of(d * size, size)
+
+    def slab_of(d):
+        return pl.ds(times(d, slab), slab)
+
+    def rows_of(d):
+        return pl.ds(times(d, rows), rows)
+
+    w_copy = pltpu.make_async_copy(w_hbm, wv, w_sem)
+    w_copy.start()
+
+    barrier = pltpu.get_barrier_semaphore()
+    for k in range(1, n):
+        pl.semaphore_signal(barrier, inc=1, device_id={"seq": (me + k) % n}, device_id_type=MESH)
+    for k in (1, pipes - 1):
+        pl.semaphore_signal(barrier, inc=1, device_id={"pipe": (pipe + k) % pipes}, device_id_type=MESH)
+    pl.semaphore_wait(barrier, n + 1)
+
+    def to_slab(phase, src, dst, d, start):
+        return pltpu.make_async_remote_copy(
+            src_ref=src.at[:, :, slab_of(d)],
+            dst_ref=dst.at[:, rows_of(start), :],
+            send_sem=a_s.at[phase, d],
+            recv_sem=a_r.at[phase, start],
+            device_id={"seq": d},
+            device_id_type=MESH,
+        )
+
+    def to_rows(phase, src, dst, d, start):
+        return pltpu.make_async_remote_copy(
+            src_ref=src.at[:, rows_of(d), :],
+            dst_ref=dst.at[:, :, slab_of(start)],
+            send_sem=a_s.at[phase, d],
+            recv_sem=a_r.at[phase, start],
+            device_id={"seq": d},
+            device_id_type=MESH,
+        )
+
+    def sums_copy(d, start):
+        return pltpu.make_async_remote_copy(
+            src_ref=mine,
+            dst_ref=small_ref.at[:, slab_of(start)],
+            send_sem=a_s.at[4, d],
+            recv_sem=a_r.at[4, start],
+            device_id={"seq": d},
+            device_id_type=MESH,
+        )
+
+    x_local = pltpu.make_async_copy(x_ref.at[:, :, my_slab], xin.at[:, my_rows, :], loc_sem.at[0])
+    x_local.start()
+    for k in range(1, n):
+        to_slab(0, x_ref, xin, (me + k) % n, me).start()
+    cot_copy = pltpu.make_async_remote_copy(
+        src_ref=inc_ref, dst_ref=cot, send_sem=cot_s, recv_sem=cot_r,
+        device_id={"pipe": (pipe + pipes - 1) % pipes}, device_id_type=MESH,
+    )
+    cot_copy.start()
+
+    angle = ang_ref[:, my_slab]
+    cosines = jnp.cos(angle)
+    sines = jnp.sin(angle)
+    weight = lw_ref[:, my_slab]
+    c_low, c_high = cosines[0:1], cosines[1:2]
+    s_low, s_high = sines[0:1], sines[1:2]
+    coef[0:1, :] = c_low
+    coef[1:2, :] = s_low
+    for l in range(levels):
+        coef[pl.ds(8 + l, 1), :] = weight[l : l + 1] * c_high
+        coef[pl.ds(8 + levels + l, 1), :] = weight[l : l + 1] * s_high
+    top_row = 8 + 2 * levels
+    coef[pl.ds(top_row, 1), :] = weight[levels : levels + 1]
+    accs[...] = jnp.zeros_like(accs)
+    pads = [max(8, 2**l) for l in range(levels)]
+    for l in range(levels):
+        for b in range(batch):
+            states[l][b, pl.ds(0, pads[l]), :] = jnp.zeros((pads[l], slab), F32)
+            adjoints[l][b, pl.ds(seq, pads[l]), :] = jnp.zeros((pads[l], slab), F32)
+    x_local.wait()
+
+    root = (2.0 / 3.141592653589793) ** 0.5
+
+    def forward(j, carry):
+        @pl.when(j != me)
+        def _():
+            to_slab(0, x_ref, xin, me, j).wait_recv()
+
+        base = times(j, rows)
+        for b in range(batch):
+            now = xin[b, pl.ds(base, rows), :].astype(F32)
+            mixed = jnp.zeros((rows, slab), F32)
+            for l in range(levels):
+                states[l][b, pl.ds(base + pads[l], rows), :] = now
+                before = states[l][b, pl.ds(base + (pads[l] - 2**l), rows), :]
+                mixed = mixed + (coef[pl.ds(8 + l, 1), :] * now + coef[pl.ds(8 + levels + l, 1), :] * before)
+                now = coef[0:1, :] * now + coef[1:2, :] * before
+            states[levels][b, pl.ds(base, rows), :] = now
+            mixed = mixed + coef[pl.ds(top_row, 1), :] * now
+            square = mixed * mixed
+            t = jnp.tanh(root * mixed * (1.0 + 0.044715 * square))
+            half = 0.5 * (1.0 + t)
+            actc[b, pl.ds(base, rows), :] = (mixed * half).astype(BF16)
+            dgelu[b, pl.ds(base, rows), :] = half + (0.5 * root) * mixed * (1.0 - t * t) * (
+                1.0 + (3.0 * 0.044715) * square
+            )
+
+        @pl.when(j != me)
+        def _():
+            to_rows(1, actc, actf, j, me).start()
+
+        return carry
+
+    lax.fori_loop(0, n, forward, 0)
+    for b in range(batch):
+        actf[b, :, my_slab] = actc[b, my_rows, :]
+    w_copy.wait()
+    cot_copy.wait_recv()
+    for k in range(1, n):
+        to_rows(1, actc, actf, me, (me + n - k) % n).wait_recv()
+
+    tile = 256
+    ga[...] = jnp.zeros_like(ga)
+
+    def mix(i, carry):
+        left = pl.ds(pl.multiple_of(i * tile, tile), tile)
+        right = pl.ds(pl.multiple_of(chans + i * tile, tile), tile)
+        act = actf[...].reshape(batch * rows, chans)
+        w_left = wv[:, left]
+        w_right = wv[:, right]
+        value = jnp.dot(act, w_left, preferred_element_type=F32)
+        gate = jnp.dot(act, w_right, preferred_element_type=F32)
+        sig = jax.nn.sigmoid(gate)
+        up = cot[:, :, left].reshape(batch * rows, tile).astype(F32) * sig
+        first = up.astype(BF16)
+        second = (up * value * (1.0 - sig)).astype(BF16)
+        gp[:, left] = first
+        gp[:, right] = second
+        dims = (((1,), (1,)), ((), ()))
+        ga[...] += lax.dot_general(first, w_left, dims, preferred_element_type=F32) + lax.dot_general(
+            second, w_right, dims, preferred_element_type=F32
+        )
+        return carry
+
+    lax.fori_loop(0, chans // tile, mix, 0)
+    gab[...] = ga[...].astype(BF16).reshape(batch, rows, chans)
+    for k in range(1, n):
+        to_slab(2, gab, gac, (me + k) % n, me).start()
+    for b in range(batch):
+        gac[b, my_rows, :] = gab[b, :, my_slab]
+
+    other = me + 1 - 2 * core
+    half_rows = chans // nz // CORES
+    theirs = pl.ds(pl.multiple_of((1 - core) * half_rows, half_rows), half_rows)
+    ours = pl.ds(pl.multiple_of(core * half_rows, half_rows), half_rows)
+
+    def pair_copy(q):
+        return pltpu.make_async_remote_copy(
+            src_ref=pb.at[q, theirs, :], dst_ref=px.at[q], send_sem=px_s.at[q], recv_sem=px_r.at[q],
+            device_id={"seq": other}, device_id_type=MESH,
+        )
+
+    width = 512
+
+    def outer_product(q, carry):
+        block = pl.ds(pl.multiple_of(q * (chans // nz), chans // nz), chans // nz)
+
+        def columns(i, carry):
+            cols = pl.ds(pl.multiple_of(i * width, width), width)
+            part = actf[:, :, block].reshape(batch * rows, chans // nz)
+            pb[q, :, cols] = lax.dot_general(
+                part, gp[:, cols], (((0,), (0,)), ((), ())), preferred_element_type=F32
+            ).astype(BF16)
+            return carry
+
+        lax.fori_loop(0, 2 * chans // width, columns, 0)
+        pair_copy(q).start()
+        return carry
+
+    lax.fori_loop(0, nz, outer_product, 0)
+
+    def chain_copy(side, q):
+        src, dst = ((txr, rxr), (txl, rxl))[side]
+        return pltpu.make_async_remote_copy(
+            src_ref=src.at[q], dst_ref=dst.at[q], send_sem=rs_s.at[side, q], recv_sem=rs_r.at[side, q],
+            device_id={"seq": (me + (CORES if side == 0 else n - CORES)) % n}, device_id_type=MESH,
+        )
+
+    def summed(q, extra, into):
+        def body(i, carry):
+            cols = pl.ds(pl.multiple_of(i * width, width), width)
+            total = pb[q, ours, cols].astype(F32) + px[q, :, cols].astype(F32)
+            for e in extra:
+                total = total + e[q, :, cols].astype(F32)
+            into[:, cols] = total.astype(into.dtype)
+            return carry
+
+        lax.fori_loop(0, 2 * chans // width, body, 0)
+
+    for q in range(nz):
+        pair_copy(q).wait_recv()
+
+    def send_step(step, ends):
+        right_q, left_q = nz - 1 - step, step
+        for side, q, goes, first in (
+            (0, right_q, z < right_q, z == 0),
+            (1, left_q, z > left_q, z == nz - 1),
+        ):
+            if ends:
+                @pl.when(jnp.logical_and(goes, first))
+                def _():
+                    summed(q, (), (txr, txl)[side].at[q])
+                    chain_copy(side, q).start()
+            else:
+                @pl.when(jnp.logical_and(goes, jnp.logical_not(first)))
+                def _():
+                    chain_copy(side, q).wait_recv()
+                    summed(q, ((rxr, rxl)[side],), (txr, txl)[side].at[q])
+                    chain_copy(side, q).start()
+
+    send_step(0, True)
+
+    def fold(values):
+        return jnp.sum(values.reshape(rows // 8, 8, slab), axis=0)
+
+    def backward(i, carry):
+        j = n - 1 - i
+
+        @pl.when(j != me)
+        def _():
+            to_slab(2, gab, gac, me, j).wait_recv()
+
+        base = times(j, rows)
+        for b in range(batch):
+            grad = gac[b, pl.ds(base, rows), :].astype(F32) * dgelu[b, pl.ds(base, rows), :]
+            accs[levels, 0] += fold(grad * states[levels][b, pl.ds(base, rows), :])
+            adj = coef[pl.ds(top_row, 1), :] * grad
+            for l in reversed(range(levels)):
+                adjoints[l][b, pl.ds(base, rows), :] = (
+                    coef[1:2, :] * adj + coef[pl.ds(8 + levels + l, 1), :] * grad
+                )
+                current = states[l][b, pl.ds(base + pads[l], rows), :]
+                before = states[l][b, pl.ds(base + (pads[l] - 2**l), rows), :]
+                accs[l, 0] += fold(grad * current)
+                accs[l, 1] += fold(grad * before)
+                accs[l, 2] += fold(adj * current)
+                accs[l, 3] += fold(adj * before)
+                carried = adjoints[l][b, pl.ds(base + 2**l, rows), :]
+                adj = coef[0:1, :] * adj + coef[pl.ds(8 + l, 1), :] * grad + carried
+            adjs[b, pl.ds(base, rows), :] = adj.astype(BF16)
+
+        @pl.when(j != me)
+        def _():
+            to_rows(3, adjs, adjf, j, me).start()
+
+        return carry
+
+    for i in range(n):
+        backward(i, 0)
+    for b in range(batch):
+        adjf[b, :, my_slab] = adjs[b, my_rows, :]
+
+    for step in range(1, nz - 1):
+        send_step(step, True)
+    for step in range(nz - 1):
+        send_step(step, False)
+
+    low_now = jnp.zeros((1, slab), F32)
+    low_back, high_now, high_back = low_now, low_now, low_now
+    mine[...] = jnp.zeros_like(mine)
+
+    def total(l, k):
+        return jnp.sum(accs[l, k], axis=0, keepdims=True)
+
+    for l in range(levels):
+        now, back = total(l, 0), total(l, 1)
+        weight_l = lw_ref[pl.ds(l, 1), my_slab]
+        mine[pl.ds(l, 1), :] = c_high * now + s_high * back
+        high_now = high_now + weight_l * now
+        high_back = high_back + weight_l * back
+        low_now = low_now + total(l, 2)
+        low_back = low_back + total(l, 3)
+    mine[pl.ds(levels, 1), :] = total(levels, 0)
+    mine[pl.ds(levels + 1, 1), :] = c_low * low_back - s_low * low_now
+    mine[pl.ds(levels + 2, 1), :] = c_high * high_back - s_high * high_now
+    for k in range(1, n):
+        sums_copy((me + k) % n, me).start()
+    small_ref[:, my_slab] = mine[...]
+
+    for k in range(1, n):
+        to_rows(3, adjs, adjf, me, (me + n - k) % n).wait_recv()
+    for b in range(batch):
+        gin_ref[b] = (cot[b].astype(F32) + adjf[b].astype(F32)).astype(BF16)
+
+    for q in range(nz):
+        @pl.when(q == z)
+        def _():
+            if q > 0:
+                chain_copy(0, q).wait_recv()
+            if q < nz - 1:
+                chain_copy(1, q).wait_recv()
+            extra = ((rxr,) if q > 0 else ()) + ((rxl,) if q < nz - 1 else ())
+            summed(q, extra, gmix_ref)
+
+    for k in range(1, n):
+        sums_copy(me, (me + n - k) % n).wait_recv()
+
+    for k in range(1, n):
+        d = (me + k) % n
+        to_slab(0, x_ref, xin, d, me).wait_send()
+        to_rows(1, actc, actf, d, me).wait_send()
+        to_slab(2, gab, gac, d, me).wait_send()
+        to_rows(3, adjs, adjf, d, me).wait_send()
+        sums_copy(d, me).wait_send()
+    cot_copy.wait_send()
+    for q in range(nz):
+        pair_copy(q).wait_send()
+
+        @pl.when(z < q)
+        def _():
+            chain_copy(0, q).wait_send()
+
+        @pl.when(z > q)
+        def _():
+            chain_copy(1, q).wait_send()
+
+
+def shards_by_slabs(pipes, n, inputs, incoming, angles, level_weights, mix_weight):
+    _, batch, rows, chans = inputs.shape
+    levels = level_weights.shape[1] - 1
+    seq = n * rows
+    slab = chans // n
+    nz = n // CORES
+    grad_scale = float(batch * seq) ** (-0.5)
+    small_rows = -(-(levels + 3) // 8) * 8
+    pads = [max(8, 2**l) for l in range(levels)]
+    vmem = pl.BlockSpec(memory_space=pltpu.VMEM)
+    grid_rows = batch * rows
+    block = (nz, chans // n, 2 * chans)
+    grad_input, small, grad_mix = pl.pallas_call(
+        functools.partial(whole_kernel, pipes, n, levels),
+        out_shape=(
+            jax.ShapeDtypeStruct((batch, rows, chans), BF16),
+            jax.ShapeDtypeStruct((small_rows, chans), F32),
+            jax.ShapeDtypeStruct((chans // n, 2 * chans), F32),
+        ),
+        in_specs=[vmem, vmem, vmem, vmem, pl.BlockSpec(memory_space=pl.ANY)],
+        out_specs=(vmem, vmem, vmem),
+        scratch_shapes=[
+            pltpu.VMEM((batch, seq, slab), BF16),
+            pltpu.VMEM((batch, rows, chans), BF16),
+            pltpu.VMEM((chans, 2 * chans), BF16),
+            pltpu.VMEM((batch, seq, slab), BF16),
+            pltpu.VMEM((batch, rows, chans), BF16),
+            pltpu.VMEM((grid_rows, 2 * chans), BF16),
+            pltpu.VMEM((grid_rows, chans), F32),
+            pltpu.VMEM((batch, rows, chans), BF16),
+            pltpu.VMEM((batch, seq, slab), BF16),
+            pltpu.VMEM((batch, seq, slab), F32),
+            pltpu.VMEM((batch, seq, slab), BF16),
+            pltpu.VMEM((batch, rows, chans), BF16),
+            pltpu.VMEM((-(-(9 + 2 * levels) // 8) * 8, slab), F32),
+            pltpu.VMEM((levels + 1, 4, 8, slab), F32),
+            pltpu.VMEM((small_rows, slab), F32),
+            pltpu.VMEM((nz, chans // nz, 2 * chans), BF16),
+            pltpu.VMEM(block, BF16),
+            pltpu.VMEM(block, BF16),
+            pltpu.VMEM(block, BF16),
+            pltpu.VMEM(block, BF16),
+            pltpu.VMEM(block, BF16),
+            [pltpu.VMEM((batch, pad + seq, slab), F32) for pad in pads + [0]],
+            [pltpu.VMEM((batch, seq + pad, slab), F32) for pad in pads],
+            pltpu.SemaphoreType.DMA,
+            pltpu.SemaphoreType.DMA,
+            pltpu.SemaphoreType.DMA,
+            pltpu.SemaphoreType.DMA((1,)),
+            pltpu.SemaphoreType.DMA((5, n)),
+            pltpu.SemaphoreType.DMA((5, n)),
+            pltpu.SemaphoreType.DMA((nz,)),
+            pltpu.SemaphoreType.DMA((nz,)),
+            pltpu.SemaphoreType.DMA((2, nz)),
+            pltpu.SemaphoreType.DMA((2, nz)),
+        ],
+        compiler_params=pltpu.CompilerParams(
+            collective_id=0, has_side_effects=True, vmem_limit_bytes=60 * 2**20
+        ),
+        cost_estimate=pl.CostEstimate(
+            flops=12 * grid_rows * chans * chans, bytes_accessed=8 * 2**20, transcendentals=4 * grid_rows * chans
+        ),
+    )(inputs[0], incoming[0], angles[0], level_weights[0], mix_weight[0])
+    return (
+        grad_input[None],
+        (small[levels + 1 : levels + 3] * grad_scale)[None],
+        (small[: levels + 1] * grad_scale)[None],
+        (grad_mix * grad_scale)[None],
+    )
+
+
+def shards_choice(pipes, n, inputs, incoming, angles, level_weights, mix_weight):
+    _, _, rows, chans = inputs.shape
+    levels = level_weights.shape[1] - 1
+    fits = chans == 128 * n and n % CORES == 0 and pipes > 2 and rows % 16 == 0 and 2**levels <= n * rows <= 1024
+    if fits:
+        return shards_by_slabs(pipes, n, inputs, incoming, angles, level_weights, mix_weight)
+    return shards_by_levels(inputs, incoming, angles, level_weights, mix_weight)
+
+
 def solution(mesh):
+    body = functools.partial(shards_choice, mesh.shape["pipe"], mesh.shape["seq"])
     placed = (
         P("pipe", None, "seq", None),
         P("pipe", None, "seq", None),
@@ -144,7 +580,7 @@
         P("pipe", None, None),
     )
     return jax.shard_map(
-        shards,
+        body,
         mesh=mesh,
         in_specs=placed,
         out_specs=(

time: 296 us -> 110 us (0.37)
  waiting for transfers between devices: 139 us -> 0 us
  Pallas kernels: 0 us -> 100 us
  starting transfers between devices: 68.5 us -> 0 us
  blocking collectives: 29.8 us -> 0 us
  other arithmetic: 26.6 us -> 4.51 us
  between operations: 15.9 us -> 0.64 us
  matrix products: 10.7 us -> 0 us
    ppermute x21 -> x0, waiting for transfers between devices: 139 us -> none  [the longest x20 139 us: shifted_2(): return lax.ppermute(block, axis, route)]
    pallas_call x0 -> x1, Pallas kernels: none -> 100 us  [shards_by_slabs(): pl.pallas_call(functools.partial(whole_kernel, pipes, n, levels), out_sha...]
    ppermute x21 -> x0, starting transfers between devices: 68.5 us -> none  [the longest x20 66 us: shifted_2(): return lax.ppermute(block, axis, route)]
    psum x1 -> x0, blocking collectives: 29.8 us -> none  [shards(): lax.psum((angle_terms, jnp.stack(level_grads)), 'seq')]
    reduce_sum x8 -> x0, other arithmetic: 11.9 us -> none  [the longest x7 8.78 us: tap_terms(): jnp.sum(adjoint * previous, axis=(0, 1))]
    dot_general x3 -> x0, matrix products: 10.7 us -> none  [the longest x1 4.96 us: shards(): jnp.einsum('rk,ck->rc', grad_proj, w_mix, preferred_element_type=jnp.floa...]
    convert_element_type x19 -> x0, other arithmetic: 9.63 us -> none  [the longest x18 5.54 us: rounded(): return lax.optimization_barrier(values.astype(jnp.bfloat16))]
    unnamed x210 -> x3, local copies, waits for them, and re-layouts: 0.6 us -> 3.96 us
  transfers between devices with their start and end apart: 22 -> 0, of which waited for: 18 -> 0; matrix products, arithmetic and copies ran while one was open for 10% -> 0% of each run, Pallas kernels for 0% -> 0%
where the time goes in v1:
time: 110 us
  Pallas kernels  100 us (91%)
  other arithmetic  4.51 us (4%)
  local copies, waits for them, and re-layouts  3.96 us (4%)
    pallas_call x1, Pallas kernels, shards_by_slabs(): pl.pallas_call(functools.partial(whole_kernel, pipes, n, levels), out_sha...  100 us
    unnamed x3, local copies, waits for them, and re-layouts  3.96 us
    broadcast_in_dim x1, other arithmetic, shards_by_slabs(): (grad_mix * grad_scale)[None]  2.3 us

profile of v1, /device:TPU:0, one launch (start us, length us, event | category | flops | bytes accessed | tf_op | source)
XLA Modules:
  0.0 109.6 jit_solution(1850793406034954366)
XLA Ops:
  0.6 1.4 %copy.12 = f32[1,11,1024]{2,1,0:T(8,128)} copy(f32[1,11,1024]{2,0,1:T(1,128)} %param.8) | data formatting | bytes 90112
  2.1 100.4 %shard_map.84 = (bf16[2,128,1024]{2,1,0:T(8,128)(2,1)}, f32[16,1024]{1,0:T(8,128)}, f32[128,2048]{1,0:T(8,128)}) custom-call(bf16[2,128,1024]{2,1,0:T(8,128)(2,1)} %bitcast.17, bf16[2,128,1024]{2,1,0:T(8,128)(2,1)} %bitcast.18, f32[2,1024]{1,0:T(2,128)} %bitcast.19, f32[11,1024]{1,0:T(8,128)} %bitcast.15, bf16[1024,2048]{1,0:T(8,128)(2,1)} %bitcast.16), custom_call_target="tpu_custom_call" | custom-call | flops 3221225472 | bytes 8388608 | tf_op jit(solution)/shard_map/pallas_call | solution.py:505
  102.5 1.4 %multiply_bitcast_fusion.2 = f32[1,2,1024]{2,1,0:T(2,128)} fusion(f32[16,1024]{1,0:T(8,128)} %get-tuple-element.8), kind=kLoop, calls=%fused_computation.3 | loop fusion | flops 2048 | bytes 16384 | tf_op jit(solution)/shard_map/broadcast_in_dim | solution.py:558
  103.9 0.8 multiply_bitcast_fusion.1
  104.7 0.7 copy.9
  105.4 2.3 %multiply_bitcast_fusion = f32[1,128,2048]{2,1,0:T(8,128)} fusion(f32[128,2048]{1,0:T(8,128)} %get-tuple-element.9), kind=kLoop, calls=%fused_computation | loop fusion | flops 262144 | bytes 2097152 | tf_op jit(solution)/shard_map/broadcast_in_dim | solution.py:560
  107.7 1.9 %copy.14 = bf16[1,2,128,1024]{3,2,1,0:T(8,128)(2,1)} copy(bf16[1,2,128,1024]{3,2,1,0:T(8,128)(2,1)} %bitcast.14) | data formatting | bytes 1048576
